TPU v7x, 256 devices: a whole 4x4x8 slice. The times are simulated.
256 devices in a mesh: dp: 32 (over z_lo, x, core), ctx: 8 (over z_hi, y).
Axes of the slice: x: 4, y: 4, z: 8 (z_hi: 2, z_lo: 4; z = z_hi * 4 + z_lo), core: 2. Of those that a mesh axis runs over, the one named last changes fastest.
Arguments:
- queries: bfloat16 [32, 1024, 4096], P('dp', 'ctx'), may hold values from -4.5 to 4.5
- keys: bfloat16 [32, 1024, 1024], P('dp', 'ctx'), may hold values from -4 to 4
- values: bfloat16 [32, 1024, 1024], P('dp', 'ctx'), may hold values from -6 to 6
- prefix_keys: bfloat16 [128, 1024], replicated, may hold values from -6 to 6
- prefix_values: bfloat16 [128, 1024], replicated, may hold values from -6 to 6
- out_grad: bfloat16 [32, 1024, 4096], P('dp', 'ctx'), may hold values from -6 to 6
- boundaries: int32 [32, 8], P('dp'), may hold values from 0 to 448, as said below
- lengths: int32 [32], P('dp'), may hold values from 512 to 1024, as said below
- advantages: float32 [32, 8], P('dp'), may hold values from -4 to 4
Outputs:
- query_grad: bfloat16 [32, 1024, 4096], P('dp', 'ctx')
- key_grad: bfloat16 [32, 1024, 1024], P('dp', 'ctx')
- value_grad: bfloat16 [32, 1024, 1024], P('dp', 'ctx')
- prefix_key_grad: float32 [128, 1024], replicated
- prefix_value_grad: float32 [128, 1024], replicated
Inputs may be any that keep to these rules, and one draw needn't show every extreme that they name: Each row begins at 0 and rises strictly; consecutive boundaries differ by at most 64. `lengths`: trajectory 0 always has length 1024.
All inputs are finite; a program needn't handle non-finite values.
Results may differ from a plain program's by a relative error of at most 0.019.
Values may be sent and summed in bfloat16 or wider, within the bound.
A program may use at most 128 MiB of HBM per device.

v0:
```python
import jax
import jax.numpy as jnp
from jax import lax
from jax.sharding import PartitionSpec as P

HEAD_DIM = 128


NEG = -1e30


def masked_scores(query, key_rows, query_pos, key_pos, score_scale):
    scores = (
        jnp.einsum("rgd,kd->grk", query, key_rows, preferred_element_type=jnp.float32) * score_scale
    )
    seen = key_pos[None, :] <= query_pos[:, None]
    return jnp.where(seen[None], scores, NEG)


def stats_update(
    query, key_rows, value_rows, query_pos, key_pos, score_scale, peak, total, weighted
):
    scores = masked_scores(query, key_rows, query_pos, key_pos, score_scale)
    new_peak = jnp.maximum(peak, jnp.max(scores, axis=-1))
    factor = jnp.exp(peak - new_peak)
    raised = jnp.exp(scores - new_peak[..., None])
    total = total * factor + jnp.sum(raised, axis=-1)
    weighted = weighted * factor[..., None] + jnp.einsum(
        "grk,kd->grd", raised.astype(jnp.bfloat16), value_rows, preferred_element_type=jnp.float32
    )
    return (new_peak, total, weighted)


def finish_stats(grad_out, peak, total, weighted):
    log_total = peak + jnp.log(total)
    attn_out = weighted / total[..., None]
    delta = jnp.einsum("rgd,grd->gr", grad_out.astype(jnp.float32), attn_out)
    return (log_total, delta)


def grad_block(
    query, grad_out, key_rows, value_rows, query_pos, key_pos, score_scale, log_total, delta
):
    scores = masked_scores(query, key_rows, query_pos, key_pos, score_scale)
    probs = jnp.exp(scores - log_total[..., None])
    probs_low = probs.astype(jnp.bfloat16)
    value_dot = jnp.einsum("rgd,kd->grk", grad_out, value_rows, preferred_element_type=jnp.float32)
    score_grad = (probs * (value_dot - delta[..., None]) * score_scale).astype(jnp.bfloat16)
    query_part = jnp.einsum("grk,kd->rgd", score_grad, key_rows, preferred_element_type=jnp.float32)
    key_part = jnp.einsum("grk,rgd->kd", score_grad, query, preferred_element_type=jnp.float32)
    value_part = jnp.einsum("grk,rgd->kd", probs_low, grad_out, preferred_element_type=jnp.float32)
    return (query_part, key_part, value_part)


def body(
    queries, keys, values, prefix_keys, prefix_values, out_grad, boundaries, lengths, advantages
):
    traj_count, rows, width = queries.shape
    kv_width = keys.shape[2]
    head_dim = HEAD_DIM
    kv_count = kv_width // head_dim
    group = width // kv_width
    items = traj_count * kv_count
    prefix_len = prefix_keys.shape[0]
    score_scale = head_dim ** (-0.5)
    ctx_count = lax.axis_size("ctx")
    place = lax.axis_index("ctx")
    steps_count = boundaries.shape[1]
    query_pos = place * rows + jnp.arange(rows, dtype=jnp.int32)
    local_pos = jnp.arange(rows, dtype=jnp.int32)
    step_of = (
        jnp.sum((boundaries[:, None, :] <= query_pos[None, :, None]).astype(jnp.int32), axis=-1) - 1
    )
    onehot = step_of[..., None] == jnp.arange(steps_count, dtype=jnp.int32)[None, None, :]
    token_weight = jnp.sum(jnp.where(onehot, advantages[:, None, :], 0.0), axis=-1)
    token_weight = jnp.where(query_pos[None, :] < lengths[:, None], token_weight, 0.0)
    weighted_grad = (out_grad.astype(jnp.float32) * token_weight[..., None]).astype(jnp.bfloat16)

    def query_items_of(array):
        shaped = array.reshape(traj_count, rows, kv_count, group, head_dim)
        return shaped.transpose(0, 2, 1, 3, 4).reshape(items, rows, group, head_dim)

    def key_items_of(array):
        length = array.shape[1]
        shaped = array.reshape(traj_count, length, kv_count, head_dim)
        return shaped.transpose(0, 2, 1, 3).reshape(items, length, head_dim)

    def key_items_back(array):
        length = array.shape[1]
        shaped = array.reshape(traj_count, kv_count, length, head_dim)
        return shaped.transpose(0, 2, 1, 3).reshape(traj_count, length, kv_width)

    def prefix_back(array):
        shaped = array.reshape(traj_count, kv_count, prefix_len, head_dim)
        return jnp.sum(shaped, axis=0).transpose(1, 0, 2).reshape(prefix_len, kv_width)

    query_items = query_items_of(queries)
    grad_items = query_items_of(weighted_grad)
    prefix_k = (
        prefix_keys.reshape(prefix_len, kv_count, head_dim)
        .transpose(1, 0, 2)[None]
        .reshape(items, prefix_len, head_dim)
    )
    prefix_v = (
        prefix_values.reshape(prefix_len, kv_count, head_dim)
        .transpose(1, 0, 2)[None]
        .reshape(items, prefix_len, head_dim)
    )
    prefix_pos = jnp.full((prefix_len,), -1, jnp.int32)

    def prefix_stats(parts):
        query, key_part, value_part = parts
        start_peak = jnp.full((group, rows), NEG, jnp.float32)
        start_total = jnp.zeros((group, rows), jnp.float32)
        start_weighted = jnp.zeros((group, rows, head_dim), jnp.float32)
        return stats_update(
            query,
            key_part,
            value_part,
            query_pos,
            prefix_pos,
            score_scale,
            start_peak,
            start_total,
            start_weighted,
        )

    def prefix_item(parts):
        return grad_block(
            parts[0],
            parts[1],
            parts[2],
            parts[3],
            query_pos,
            prefix_pos,
            score_scale,
            parts[4],
            parts[5],
        )

    peak, total, weighted = lax.map(prefix_stats, (query_items, prefix_k, prefix_v))
    key_all, value_all = (
        lax.all_gather(keys, "ctx", axis=1, tiled=True),
        lax.all_gather(values, "ctx", axis=1, tiled=True),
    )
    key_parts = key_items_of(key_all).reshape(items, ctx_count, rows, head_dim)
    value_parts = key_items_of(value_all).reshape(items, ctx_count, rows, head_dim)

    def stat_piece(index, carry):
        key_pos = index * rows + local_pos
        block_k = lax.dynamic_index_in_dim(key_parts, index, 1, keepdims=False)
        block_v = lax.dynamic_index_in_dim(value_parts, index, 1, keepdims=False)

        def stat_active(state):

            def item_stats(parts):
                return stats_update(
                    parts[0],
                    parts[1],
                    parts[2],
                    query_pos,
                    key_pos,
                    score_scale,
                    parts[3],
                    parts[4],
                    parts[5],
                )

            return lax.map(
                item_stats, (query_items, block_k, block_v, state[0], state[1], state[2])
            )

        return lax.cond(index <= place, stat_active, lambda state: state, carry)

    peak, total, weighted = lax.fori_loop(0, ctx_count, stat_piece, (peak, total, weighted))
    log_total, delta = jax.vmap(finish_stats)(grad_items, peak, total, weighted)
    query_grad_items, prefix_key_items, prefix_value_items = lax.map(
        prefix_item, (query_items, grad_items, prefix_k, prefix_v, log_total, delta)
    )
    prefix_key_part = prefix_back(prefix_key_items)
    prefix_value_part = prefix_back(prefix_value_items)

    def grad_piece(index, carry):
        key_pos = index * rows + local_pos
        block_k = lax.dynamic_index_in_dim(key_parts, index, 1, keepdims=False)
        block_v = lax.dynamic_index_in_dim(value_parts, index, 1, keepdims=False)

        def grad_active(state):
            query_total, key_store, value_store = state

            def item_grads(parts):
                return grad_block(
                    parts[0],
                    parts[1],
                    parts[2],
                    parts[3],
                    query_pos,
                    key_pos,
                    score_scale,
                    parts[4],
                    parts[5],
                )

            query_part, key_part, value_part = lax.map(
                item_grads, (query_items, grad_items, block_k, block_v, log_total, delta)
            )
            key_store = lax.dynamic_update_index_in_dim(key_store, key_part, index, 1)
            value_store = lax.dynamic_update_index_in_dim(value_store, value_part, index, 1)
            return (query_total + query_part, key_store, value_store)

        return lax.cond(index <= place, grad_active, lambda state: state, carry)

    zero_store = jnp.zeros((items, ctx_count, rows, head_dim), jnp.float32)
    query_grad_items, key_store, value_store = lax.fori_loop(
        0, ctx_count, grad_piece, (query_grad_items, zero_store, zero_store)
    )
    key_terms = key_items_back(key_store.reshape(items, ctx_count * rows, head_dim))
    value_terms = key_items_back(value_store.reshape(items, ctx_count * rows, head_dim))
    key_sum, value_sum = (
        lax.psum_scatter(
            key_terms.astype(jnp.bfloat16), "ctx", scatter_dimension=1, tiled=True
        ).astype(jnp.float32),
        lax.psum_scatter(
            value_terms.astype(jnp.bfloat16), "ctx", scatter_dimension=1, tiled=True
        ).astype(jnp.float32),
    )
    query_grad = (
        query_grad_items.reshape(traj_count, kv_count, rows, group, head_dim)
        .transpose(0, 2, 1, 3, 4)
        .reshape(traj_count, rows, width)
    )
    prefix_key_grad, prefix_value_grad = lax.psum(
        (prefix_key_part, prefix_value_part), ("dp", "ctx")
    )
    return (
        query_grad.astype(jnp.bfloat16),
        key_sum.astype(jnp.bfloat16),
        value_sum.astype(jnp.bfloat16),
        prefix_key_grad,
        prefix_value_grad,
    )


def solution(mesh):
    in_specs = (
        P("dp", "ctx", None),
        P("dp", "ctx", None),
        P("dp", "ctx", None),
        P(),
        P(),
        P("dp", "ctx", None),
        P("dp", None),
        P("dp"),
        P("dp", None),
    )
    out_specs = (P("dp", "ctx", None), P("dp", "ctx", None), P("dp", "ctx", None), P(), P())
    return jax.shard_map(body, mesh=mesh, in_specs=in_specs, out_specs=out_specs, check_vma=False)
```

profile of v0, /device:TPU:1, one launch (start us, length us, event | category | flops | bytes accessed | tf_op | source)
XLA Modules:
  0.0 1037.7 jit_solution(8061411740984875714)
XLA Ops:
  7.2 1.9 copy.138
  9.2 1.8 copy.140
  11.1 1.1 copy.132
  14.1 10.1 while.134
  15.7 1.0 fusion.173
  17.0 1.0 fusion.173
  27.3 1.7 copy.173
  29.0 61.6 %all-gather.3.cloned.1.call-done = bf16[1,1024,1024]{1,2,0:T(8,128)(2,1)} async-done(((bf16[1,128,1024]{1,2,0:T(8,128)(2,1)}), bf16[1,1024,1024]{1,2,0:T(8,128)(2,1)}) %all-gather.3.cloned.1.call-update) | async-done | bytes 2097168 | tf_op jit(solution)/shard_map/all_gather | solution.py:143
  90.7 3.9 copy.139
  94.6 3.2 copy.142
  97.8 68.8 %all-gather.5.cloned.1.call-done = bf16[1,1024,1024]{1,2,0:T(8,128)(2,1)} async-done(((bf16[1,128,1024]{1,2,0:T(8,128)(2,1)}), bf16[1,1024,1024]{1,2,0:T(8,128)(2,1)}) %all-gather.5.cloned.1.call-update) | async-done | bytes 2097168 | tf_op jit(solution)/shard_map/all_gather | solution.py:144
  166.5 3.9 copy.141
  170.5 3.1 copy.143
  173.6 23.0 %while.135 = (s32[]{:T(128)}, f32[8,4,128]{2,1,0:T(4,128)S(1)}, f32[8,4,128]{2,1,0:T(4,128)S(1)}, f32[8,4,128,128]{3,2,1,0:T(8,128)}, s32[]{:T(128)}, /*index=5*...) while((s32[]{:T(128)}, f32[8,4,128]{2,1,0:T(4,128)S(1)}, ...), condition=%wide.region_13.14_spmd.clone, body=%wide.region_6.13_spmd.clone.sunk | while | flops 34162948 | bytes 6885400 | solution.py:175
  173.6 22.7 %conditional.6 = ((f32[8,4,128]{2,1,0:T(4,128)S(1)}, f32[8,4,128]{2,1,0:T(4,128)S(1)}, f32[8,4,128,128]{3,2,1,0:T(8,128)})) conditional(s32[]{:T(128)} %convert_element_type.158, (f32[8,4,128]{2,1,0:T(4,128)S(1)}, f32[8,4,128]{2,1,0:T(4,128)S(1)}, f32[8,4,128,128]{3,2,1,0:T(8,128)}) %tuple.203, (bf16[8,8,128,128]{3,2,0,1:T(8,128)(2,1)}, s32[]{:T(128)}, ...), branch_computations={%region_7.7_spmd, %region_8.12_spmd} | conditional | flops 34162944 | bytes 6884661 | solution.py:173
  173.6 1.1 dynamic-slice_bitcast_fusion
  174.7 18.4 %while.132 = (s32[]{:T(128)}, f32[8,4,128]{2,1,0:T(4,128)S(1)}, f32[8,4,128]{2,1,0:T(4,128)S(1)}, f32[8,4,128,128]{3,2,1,0:T(8,128)}, f32[8,4,128]{2,1,0:T(4,128...) while((s32[]{:T(128)}, f32[8,4,128]{2,1,0:T(4,128)S(1)}, ...), condition=%wide.region_12.11_spmd, body=%wide.region_9.10_spmd.sunk | while | flops 34162688 | bytes 1574029 | solution.py:169
  175.1 1.9 fusion.211
  177.4 1.9 fusion.211
  179.7 1.9 fusion.211
  182.0 1.9 fusion.211
  184.3 1.9 fusion.211
  186.6 1.9 fusion.211
  188.9 1.9 fusion.211
  191.2 1.9 fusion.211
  193.1 3.2 copy.246
  196.6 2.8 multiply_reduce_fusion
  199.5 29.9 %while.136 = (s32[]{:T(128)}, f32[8,128,4,128]{1,3,2,0:T(8,128)}, f32[8,128,128]{2,1,0:T(8,128)}, f32[8,128,128]{2,1,0:T(8,128)}, bf16[8,128,128]{2,1,0:T(8,128)...) while((s32[]{:T(128)}, f32[8,128,4,128]{1,3,2,0:T(8,128)}, ...), condition=%wide.region_15.16_spmd.clone, body=%wide.region_14.15_spmd.clone.sunk | while | flops 84410624 | bytes 2213637 | solution.py:177
  199.7 1.0 fusion.186
  200.7 0.9 fusion.187
  203.5 1.0 fusion.186
  207.2 1.0 fusion.186
  211.0 1.0 fusion.186
  214.7 1.0 fusion.186
  218.5 1.0 fusion.186
  222.2 1.0 fusion.186
  225.9 1.0 fusion.186
  229.4 1.9 broadcast_in_dim.173
  231.3 1.9 broadcast_in_dim.173.clone
  233.2 21.9 %while.137 = (s32[]{:T(128)}, f32[8,128,4,128]{1,3,2,0:T(8,128)}, bf16[8,8,128,128]{3,2,0,1:T(8,128)(2,1)}, bf16[8,8,128,128]{3,2,0,1:T(8,128)(2,1)}, s32[]{:T(1...) while((s32[]{:T(128)}, f32[8,128,4,128]{1,3,2,0:T(8,128)}, ...), condition=%wide.region_21.22_spmd.clone, body=%wide.region_16.21_spmd.clone.sunk | while | flops 84951296 | bytes 10638446 | solution.py:214
  233.2 21.6 %conditional.7 = ((f32[8,128,4,128]{1,3,2,0:T(8,128)}, bf16[8,8,128,128]{3,2,0,1:T(8,128)(2,1)}, bf16[8,8,128,128]{3,2,0,1:T(8,128)(2,1)})) conditional(s32[]{:T(128)} %convert_element_type.161, (f32[8,128,4,128]{1,3,2,0:T(8,128)}, bf16[8,8,128,128]{3,2,0,1:T(8,128)(2,1)}, bf16[8,8,128,128]{3,2,0,1:T(8,128)(2,1)}) %tuple.208, ...), branch_computations={%region_17.17_spmd, %region_18.20_spmd} | conditional | flops 84951296 | bytes 10637659 | solution.py:211
  233.2 1.0 dynamic-slice_bitcast_fusion.3
  234.2 1.0 dynamic-slice_bitcast_fusion.2
  235.2 14.9 %while.133 = (s32[]{:T(128)}, f32[8,128,4,128]{1,3,2,0:T(8,128)}, bf16[8,128,128]{2,1,0:T(8,128)(2,1)S(1)}, bf16[8,128,128]{2,1,0:T(8,128)(2,1)S(1)}, bf16[8,128...) while((s32[]{:T(128)}, f32[8,128,4,128]{1,3,2,0:T(8,128)}, ...), condition=%wide.region_20.19_spmd, body=%wide.region_19.18_spmd.sunk | while | flops 84426752 | bytes 2246793 | solution.py:204
  250.1 3.9 add.171
  255.1 3.2 copy.194
  258.3 2.9 copy.156
  261.1 7.7 copy.177
  268.8 4.4 copy.196
  273.3 1.5 copy-done.1
  274.8 1.5 copy.193
  276.3 2.9 copy.158
  279.1 7.7 copy.179
  286.8 4.4 copy.195
  291.3 1.0 copy-done.5
  292.4 1.1 copy_bitcast_fusion.2
  293.7 1.3 copy.175
  295.0 378.9 %reduce-scatter.7.cloned.1.call-done = bf16[128,1024]{1,0:T(8,128)(2,1)} async-done(((bf16[1024,1024]{1,0:T(8,128)(2,1)}), bf16[128,1024]{1,0:T(8,128)(2,1)}) %reduce-scatter.7.cloned.1.call-update) | async-done | bytes 262160
  673.9 1.2 reshape_bitcast_fusion.1
  676.0 93.6 %reduce-scatter.9.cloned.1.call-done = bf16[128,1024]{1,0:T(8,128)(2,1)} async-done(((bf16[1024,1024]{1,0:T(8,128)(2,1)}), bf16[128,1024]{1,0:T(8,128)(2,1)}) %reduce-scatter.9.cloned.1.call-update) | async-done | bytes 262160
  769.5 1.2 reshape_bitcast_fusion
  771.5 255.9 %all-reduce.3.cloned.1.call-done = (f32[128,1024]{1,0:T(8,128)}, f32[128,1024]{1,0:T(8,128)}) async-done(((f32[128,1024]{1,0:T(8,128)}, f32[128,1024]{1,0:T(8,128)}), (f32[128,1024]{1,0:T(8,128)}, f32[128,1024]{1,0:T(8,128)})) %all-reduce.3.cloned.1.call-update) | async-done | bytes 1048592 | tf_op jit(solution)/shard_map/psum | solution.py:232
  1027.4 1.9 copy.302
  1029.3 1.9 copy.303
  (282 shorter events, 54.4 us)
Async XLA Ops:
  7.2 5.2 copy-start.3
  7.2 83.5 %all-gather.3.cloned.1.call-start = ((), (), s32[]{:S(2)}) async-start(), calls=%async_computation.2 | async-start | bytes 2359296 | tf_op jit(solution)/shard_map/all_gather | solution.py:143
  9.1 157.4 %all-gather.5.cloned.1.call-start = ((), (), s32[]{:S(2)}) async-start(), calls=%async_computation.3 | async-start | bytes 2359296 | tf_op jit(solution)/shard_map/all_gather | solution.py:144
  11.0 663.0 %reduce-scatter.7.cloned.1.call-start = ((), (), s32[]{:S(2)}) async-start(), calls=%async_computation.4 | async-start | bytes 2359296
  12.4 1.4 copy-start.7
  14.1 10.8 %copy-start.4 = (bf16[1,128,4096]{2,1,0:T(8,128)(2,1)S(1)}, bf16[1,128,4096]{2,1,0:T(8,128)(2,1)}, u32[]{:S(2)}) copy-start(bf16[1,128,4096]{2,1,0:T(8,128)(2,1)} %param.30) | copy-start | bytes 3145732
  24.2 0.7 copy-start.2
  24.2 2.0 copy-start.8
  24.2 2.1 copy-start.9
  273.2 1.6 copy-start.1
  273.2 496.3 %reduce-scatter.9.cloned.1.call-start = ((), (), s32[]{:S(2)}) async-start(), calls=%async_computation.5 | async-start | bytes 2359296
  291.2 1.0 copy-start.5
  291.2 1.2 copy-start.6
  291.3 2.3 copy-start
  291.3 736.1 %all-reduce.3.cloned.1.call-start = ((), (), s32[]{:S(2)}) async-start(), calls=%async_computation.6 | async-start | bytes 2097152 | tf_op jit(solution)/shard_map/psum | solution.py:232
Sparse Core Ops, SparseCore 0:
  11.1 79.5 all-gather.2
  93.7 72.7 all-gather.4
  273.4 400.5 reduce-scatter.6
  678.4 91.0 reduce-scatter.8
  775.5 251.8 all-reduce.2
where the time goes:
time: 1040 us
  waiting for transfers between devices  859 us (83%)
  local copies, waits for them, and re-layouts  82.8 us (8%)
  matrix products  69.3 us (7%)
  between operations  14.7 us (1%)
    unnamed x7, waiting for transfers between devices  473 us
    psum x1, waiting for transfers between devices, body(): lax.psum((prefix_key_part, prefix_value_part), ('dp', 'ctx'))  256 us
    all_gather x1, waiting for transfers between devices, body(): lax.all_gather(values, 'ctx', axis=1, tiled=True)  68.8 us
    all_gather x1, waiting for transfers between devices, body(): lax.all_gather(keys, 'ctx', axis=1, tiled=True)  61.6 us
    unnamed x43, local copies, waits for them, and re-layouts  51.3 us
    dot_general x16, matrix products, stats_update(): jnp.einsum('grk,kd->grd', raised.astype(jnp.bfloat16), value_rows, prefer...  22.5 us
  transfers between devices with their start and end apart: 5, of which 5 were waited for; matrix products, arithmetic and copies ran while one was open for 5% of the time, Pallas kernels for 0%

commit v1 on v0

v1 whole, which is shorter than its diff:
```python
import functools

import jax
import jax.numpy as jnp
from jax import lax
from jax.experimental import pallas as pl
from jax.experimental.pallas import tpu as pltpu
from jax.sharding import PartitionSpec as P

HEADS = 32
KV_HEADS = 8
GROUP = HEADS // KV_HEADS
HEAD_DIM = 128
PREFIX = 128
ROWS = 128
STEPS = 8
SCALE = HEAD_DIM**-0.5
SCALE_LOG2 = SCALE * 1.4426950408889634
NEG = -1e30
MESH = pl.DeviceIdType.MESH
F32 = jnp.float32
BF16 = jnp.bfloat16
CONTRACT_LAST = (((1,), (1,)), ((), ()))
CONTRACT_FIRST = (((0,), (0,)), ((), ()))
CONTRACT_INNER = (((1,), (0,)), ((), ()))


def head_grads(h, ctx, keys_seen, unmasked, q_ref, og_ref, weight, kv, dkv, dq_ref, s_ref, d_ref):
    width = GROUP * HEAD_DIM
    cols = [pl.ds(pl.multiple_of(h * width + g * HEAD_DIM, HEAD_DIM), HEAD_DIM) for g in range(GROUP)]
    queries = jnp.concatenate([q_ref[:, c] for c in cols], axis=0)
    grads = jnp.concatenate(
        [(og_ref[:, c].astype(F32) * weight[...]).astype(BF16) for c in cols], axis=0
    )
    key_rows = kv[0, h, 0:keys_seen]
    value_rows = kv[1, h, 0:keys_seen]
    scores = lax.dot_general(key_rows, queries, CONTRACT_LAST, preferred_element_type=F32)
    query_pos = ctx * ROWS + lax.broadcasted_iota(jnp.int32, (1, ROWS), 1)
    query_pos = jnp.concatenate([query_pos] * GROUP, axis=1)
    key_pos = unmasked - PREFIX + lax.broadcasted_iota(jnp.int32, (keys_seen - unmasked, 1), 0)
    free, bound = scores[0:unmasked], scores[unmasked:]
    bound = jnp.where(key_pos <= query_pos, bound, NEG)
    s_ref[0:unmasked] = free
    s_ref[unmasked:keys_seen] = bound
    peak = jnp.maximum(
        jnp.max(free, axis=0, keepdims=True), jnp.max(bound, axis=0, keepdims=True)
    )
    d_ref[0:keys_seen] = lax.dot_general(value_rows, grads, CONTRACT_LAST, preferred_element_type=F32)
    raised = jnp.exp2((s_ref[0:keys_seen] - peak) * SCALE_LOG2)
    s_ref[0:keys_seen] = raised
    total = jnp.sum(raised, axis=0, keepdims=True)
    inverse = 1.0 / total
    delta = jnp.sum(raised * d_ref[0:keys_seen], axis=0, keepdims=True) * inverse
    probs = s_ref[0:keys_seen] * inverse
    score_grad = (probs * (d_ref[0:keys_seen] - delta)).astype(BF16)
    value_part = lax.dot_general(probs.astype(BF16), grads, CONTRACT_INNER, preferred_element_type=F32)
    dkv[1, h, 0:keys_seen] = value_part.astype(BF16)
    key_part = lax.dot_general(score_grad, queries, CONTRACT_INNER, preferred_element_type=F32)
    dkv[0, h, 0:keys_seen] = (key_part * SCALE).astype(BF16)
    query_part = lax.dot_general(key_rows, score_grad, CONTRACT_FIRST, preferred_element_type=F32)
    for g in range(GROUP):
        dq_ref[:, cols[g]] = (query_part[:, g * ROWS : (g + 1) * ROWS].T * SCALE).astype(BF16)


def kernel(
    q_ref, k_ref, v_ref, pk_ref, pv_ref, og_ref, bounds_ref, len_ref, adv_ref,
    dq_ref, dk_ref, dv_ref, dpk_ref, dpv_ref,
    kv, dkv, rb, zsum, s_ref, d_ref, weight,
    pbuf, acc, ybuf, part, zbuf, piece, part2, fin, pgb,
    kv_send, kv_recv, g_send, g_recv, p_send, p_recv,
    y_send, y_recv, z_send, z_recv, za_send, za_recv, ya_send, ya_recv, f_send, f_recv,
):
    dp = lax.axis_index("dp")
    ctx = lax.axis_index("ctx")
    y = ctx % 4
    hi = ctx // 4
    z = hi * 4 + dp // 8
    own = dp % 8
    base = dp - own

    def at_ctx(target):
        return (dp, target)

    def at_own(target):
        return (base + target, ctx)

    def at_z(target):
        return ((target % 4) * 8 + own, (target // 4) * 4 + y)

    barrier = pltpu.get_barrier_semaphore()
    for step in range(1, 8):
        pl.semaphore_signal(barrier, inc=1, device_id=at_ctx((ctx + step) % 8), device_id_type=MESH)
        pl.semaphore_signal(barrier, inc=1, device_id=at_own((own + step) % 8), device_id_type=MESH)
        if step != 4:
            pl.semaphore_signal(barrier, inc=1, device_id=at_z((z + step) % 8), device_id_type=MESH)

    def copy(src, dst, send, recv, target):
        return pltpu.make_async_remote_copy(
            src_ref=src, dst_ref=dst, send_sem=send, recv_sem=recv, device_id=target, device_id_type=MESH
        )

    def block(ref, h, j):
        return ref.at[:, h, pl.ds(pl.multiple_of((1 + j) * ROWS, ROWS), ROWS)]

    mine = pl.ds(pl.multiple_of((1 + ctx) * ROWS, ROWS), ROWS)
    for h in range(KV_HEADS):
        cols = slice(h * HEAD_DIM, (h + 1) * HEAD_DIM)
        kv[0, h, mine] = k_ref[:, cols]
        kv[1, h, mine] = v_ref[:, cols]
        kv[0, h, 0:PREFIX] = pk_ref[:, cols]
        kv[1, h, 0:PREFIX] = pv_ref[:, cols]
    for j in range(1, 8):

        @pl.when(jnp.logical_and(ctx < j, ctx // 4 == j // 4))
        def _(j=j):
            for h in range(KV_HEADS):
                kv[:, h, (1 + j) * ROWS : (2 + j) * ROWS] = jnp.zeros((2, ROWS, HEAD_DIM), BF16)

    pos = ctx * ROWS + lax.broadcasted_iota(jnp.int32, (ROWS, HEAD_DIM), 0)
    token = jnp.full((ROWS, HEAD_DIM), adv_ref[0, 0], F32)
    for s in range(1, STEPS):
        token = jnp.where(pos >= bounds_ref[0, s], adv_ref[0, s], token)
    weight[...] = jnp.where(pos < len_ref[0], token, 0.0)

    pl.semaphore_wait(barrier, 20)

    def own_copy(h, dy):
        target = hi * 4 + (y + dy) % 4
        return copy(
            block(kv, h, ctx), block(kv, h, ctx), kv_send.at[h, dy - 1], kv_recv.at[h, ctx], at_ctx(target)
        ), y + dy < 4

    def cross_copy(h):
        return copy(block(kv, h, ctx), block(kv, h, ctx), kv_send.at[h, 3], kv_recv.at[h, ctx], at_ctx(4 + y))

    def pass_copy(h, dy):
        return copy(
            block(kv, h, y), block(kv, h, y), kv_send.at[h, 2 + dy], kv_recv.at[h, y], at_ctx(4 + (y + dy) % 4)
        )

    def kv_arrived(h, j):
        copy(block(kv, h, j), block(kv, h, j), kv_send.at[h, 0], kv_recv.at[h, j], at_ctx(ctx)).wait_recv()

    def lo_term_copy(h, dy):
        target = (y + dy) % 4
        return copy(
            block(dkv, h, target), rb.at[3 - dy, :, h], g_send.at[h, dy - 1], g_recv.at[h, 3 - dy], at_ctx(4 + target)
        )

    def owner_term_copy(h, dy):
        target = (y + dy) % 4
        return copy(
            block(dkv, h, hi * 4 + target),
            rb.at[6 - dy, :, h],
            g_send.at[h, 2 + dy],
            g_recv.at[h, 6 - dy],
            at_ctx(hi * 4 + target),
        ), y + dy >= 4

    def back_copy(h):
        return copy(zsum.at[:, h], rb.at[0, :, h], g_send.at[h, 6], g_recv.at[h, 0], at_ctx(y))

    def term_arrived(h, slot):
        copy(zsum.at[:, h], rb.at[slot, :, h], g_send.at[h, 0], g_recv.at[h, slot], at_ctx(ctx)).wait_recv()

    def prefix_copy(h):
        slot = jnp.minimum((own - h + 7) % 8, 6)
        return copy(
            dkv.at[:, h, pl.ds(0, PREFIX)], pbuf.at[slot], p_send.at[h], p_recv.at[slot], at_own(h)
        ), own != h

    def when(pair, act):
        made, cond = pair
        pl.when(cond)(functools.partial(act, made))

    def start(made):
        made.start()

    def wait_send(made):
        made.wait_send()

    grads = functools.partial(
        head_grads, q_ref=q_ref, og_ref=og_ref, weight=weight, kv=kv, dkv=dkv, dq_ref=dq_ref, s_ref=s_ref, d_ref=d_ref
    )

    def send_terms(h):
        for dy in (1, 2, 3):
            when(owner_term_copy(h, dy), start)
        when(prefix_copy(h), start)

    @pl.when(hi == 0)
    def _():
        def send(h, c):
            cross_copy(h).start()
            for dy in (1, 2, 3):
                when(own_copy(h, dy), start)
            return c

        lax.fori_loop(0, KV_HEADS, send, 0)

        def step(h, c):
            for j in range(3):
                pl.when(j < ctx)(functools.partial(kv_arrived, h, j))
            grads(h, ctx, 5 * ROWS, PREFIX)
            send_terms(h)
            return c

        lax.fori_loop(0, KV_HEADS, step, 0)

    @pl.when(hi == 1)
    def _():
        def forward(h):
            for dy in (1, 2, 3):
                when(own_copy(h, dy), start)
            kv_arrived(h, y)
            for dy in (1, 2, 3):
                pass_copy(h, dy).start()

        def relay(h):
            for slot in range(3):
                term_arrived(h, slot)
            mine_too = dkv[:, h, pl.ds(pl.multiple_of((1 + y) * ROWS, ROWS), ROWS)].astype(F32)
            summed = mine_too + rb[0, :, h].astype(F32) + rb[1, :, h].astype(F32) + rb[2, :, h].astype(F32)
            zsum[:, h] = summed.astype(BF16)
            back_copy(h).start()

        forward(0)

        def step(h, c):
            pl.when(h + 1 < KV_HEADS)(lambda: forward(h + 1))
            for dy in (1, 2, 3):
                kv_arrived(h, (y + dy) % 4)
            for j in range(4, 7):
                pl.when(j < ctx)(functools.partial(kv_arrived, h, j))
            grads(h, ctx, 9 * ROWS, 5 * ROWS)
            for dy in (1, 2, 3):
                lo_term_copy(h, dy).start()
            send_terms(h)
            pl.when(h >= 1)(lambda: relay(h - 1))
            return c

        lax.fori_loop(0, KV_HEADS, step, 0)
        relay(KV_HEADS - 1)

    for slot in range(7):
        copy(pbuf.at[slot], pbuf.at[slot], p_send.at[0], p_recv.at[slot], at_own(own)).wait_recv()
    total = dkv[:, own, 0:PREFIX].astype(F32)
    for slot in range(7):
        total = total + pbuf[slot].astype(F32)
    acc[...] = total.reshape(2 * PREFIX, HEAD_DIM)

    def quarter(ref, i):
        return ref.at[pl.ds(pl.multiple_of(i * 64, 64), 64)]

    def eighth(ref, i):
        return ref.at[pl.ds(pl.multiple_of(i * 8, 8), 8)]

    ys = [
        copy(quarter(acc, (y + d) % 4), ybuf.at[3 - d], y_send.at[d - 1], y_recv.at[3 - d], at_ctx(hi * 4 + (y + d) % 4))
        for d in (1, 2, 3)
    ]
    for c in ys:
        c.start()
    for c in ys:
        c.wait_recv()
    part[...] = acc[pl.ds(pl.multiple_of(y * 64, 64), 64)] + ybuf[0] + ybuf[1] + ybuf[2]
    zs = [
        copy(eighth(part, (z + d) % 8), zbuf.at[7 - d], z_send.at[d - 1], z_recv.at[7 - d], at_z((z + d) % 8))
        for d in range(1, 8)
    ]
    for c in zs:
        c.start()
    for c in zs:
        c.wait_recv()
    total = part[pl.ds(pl.multiple_of(z * 8, 8), 8)]
    for slot in range(7):
        total = total + zbuf[slot]
    piece[...] = total
    part2[pl.ds(pl.multiple_of(z * 8, 8), 8)] = total
    zas = [
        copy(piece, eighth(part2, z), za_send.at[d - 1], za_recv.at[7 - d], at_z((z + d) % 8)) for d in range(1, 8)
    ]
    for c in zas:
        c.start()
    for d in range(1, 8):
        copy(piece, eighth(part2, (z + d) % 8), za_send.at[d - 1], za_recv.at[d - 1], at_z(z)).wait_recv()
    fin[pl.ds(pl.multiple_of(y * 64, 64), 64)] = part2[...]
    yas = [
        copy(part2, quarter(fin, y), ya_send.at[d - 1], ya_recv.at[3 - d], at_ctx(hi * 4 + (y + d) % 4))
        for d in (1, 2, 3)
    ]
    for c in yas:
        c.start()
    for d in (1, 2, 3):
        copy(part2, quarter(fin, (y + d) % 4), ya_send.at[d - 1], ya_recv.at[d - 1], at_ctx(ctx)).wait_recv()
    pgb[own] = fin[...].astype(BF16)
    fs = [
        copy(pgb.at[own], pgb.at[own], f_send.at[d - 1], f_recv.at[7 - d], at_own((own + d) % 8)) for d in range(1, 8)
    ]
    for c in fs:
        c.start()

    @pl.when(hi == 0)
    def _():
        def finish(h, c):
            term_arrived(h, 0)
            return c

        lax.fori_loop(0, KV_HEADS, finish, 0)

    @pl.when(hi == 1)
    def _():
        rb[0] = jnp.zeros(rb.shape[1:], BF16)

    for dy in (1, 2, 3):

        @pl.when(y + dy < 4)
        def _(dy=dy):
            def finish(h, c):
                term_arrived(h, 2 + dy)
                return c

            lax.fori_loop(0, KV_HEADS, finish, 0)

        @pl.when(y + dy >= 4)
        def _(dy=dy):
            rb[2 + dy] = jnp.zeros(rb.shape[1:], BF16)

    for h in range(KV_HEADS):
        total = dkv[:, h, mine].astype(F32)
        for slot in (0, 3, 4, 5):
            total = total + rb[slot, :, h].astype(F32)
        cols = slice(h * HEAD_DIM, (h + 1) * HEAD_DIM)
        dk_ref[:, cols] = total[0].astype(BF16)
        dv_ref[:, cols] = total[1].astype(BF16)

    for d in range(1, 8):
        there = (own + d) % 8
        copy(pgb.at[there], pgb.at[there], f_send.at[0], f_recv.at[d - 1], at_own(own)).wait_recv()
    for h in range(KV_HEADS):
        cols = slice(h * HEAD_DIM, (h + 1) * HEAD_DIM)
        dpk_ref[:, cols] = pgb[h, 0:PREFIX].astype(F32)
        dpv_ref[:, cols] = pgb[h, PREFIX:].astype(F32)

    for c in ys + zs + zas + yas + fs:
        c.wait_send()

    def drain(h, c):
        for dy in (1, 2, 3):
            when(own_copy(h, dy), wait_send)
            when(owner_term_copy(h, dy), wait_send)
        when(prefix_copy(h), wait_send)

        @pl.when(hi == 0)
        def _():
            cross_copy(h).wait_send()

        @pl.when(hi == 1)
        def _():
            for dy in (1, 2, 3):
                pass_copy(h, dy).wait_send()
                lo_term_copy(h, dy).wait_send()
            back_copy(h).wait_send()

        return c

    lax.fori_loop(0, KV_HEADS, drain, 0)


def body(queries, keys, values, prefix_keys, prefix_values, out_grad, boundaries, lengths, advantages):
    width, kv_width = queries.shape[2], keys.shape[2]
    vmem = pl.BlockSpec(memory_space=pltpu.VMEM)
    smem = pl.BlockSpec(memory_space=pltpu.SMEM)
    dma = pltpu.SemaphoreType.DMA
    key_rows = PREFIX + 8 * ROWS
    outs = pl.pallas_call(
        kernel,
        out_shape=[
            jax.ShapeDtypeStruct((ROWS, width), BF16),
            jax.ShapeDtypeStruct((ROWS, kv_width), BF16),
            jax.ShapeDtypeStruct((ROWS, kv_width), BF16),
            jax.ShapeDtypeStruct((PREFIX, kv_width), F32),
            jax.ShapeDtypeStruct((PREFIX, kv_width), F32),
        ],
        in_specs=[vmem] * 6 + [smem] * 3,
        out_specs=[vmem] * 5,
        scratch_shapes=[
            pltpu.VMEM((2, KV_HEADS, key_rows, HEAD_DIM), BF16),
            pltpu.VMEM((2, KV_HEADS, key_rows, HEAD_DIM), BF16),
            pltpu.VMEM((6, 2, KV_HEADS, ROWS, HEAD_DIM), BF16),
            pltpu.VMEM((2, KV_HEADS, ROWS, HEAD_DIM), BF16),
            pltpu.VMEM((key_rows, GROUP * ROWS), F32),
            pltpu.VMEM((key_rows, GROUP * ROWS), F32),
            pltpu.VMEM((ROWS, HEAD_DIM), F32),
            pltpu.VMEM((7, 2, PREFIX, HEAD_DIM), BF16),
            pltpu.VMEM((2 * PREFIX, HEAD_DIM), F32),
            pltpu.VMEM((3, 64, HEAD_DIM), F32),
            pltpu.VMEM((64, HEAD_DIM), F32),
            pltpu.VMEM((7, 8, HEAD_DIM), F32),
            pltpu.VMEM((8, HEAD_DIM), F32),
            pltpu.VMEM((64, HEAD_DIM), F32),
            pltpu.VMEM((2 * PREFIX, HEAD_DIM), F32),
            pltpu.VMEM((KV_HEADS, 2 * PREFIX, HEAD_DIM), BF16),
            dma((KV_HEADS, 6)),
            dma((KV_HEADS, 8)),
            dma((KV_HEADS, 7)),
            dma((KV_HEADS, 6)),
            dma((KV_HEADS,)),
            dma((7,)),
            dma((3,)),
            dma((3,)),
            dma((7,)),
            dma((7,)),
            dma((7,)),
            dma((7,)),
            dma((3,)),
            dma((3,)),
            dma((7,)),
            dma((7,)),
        ],
        compiler_params=pltpu.CompilerParams(
            collective_id=0, has_side_effects=True, vmem_limit_bytes=56 * 2**20
        ),
        cost_estimate=pl.CostEstimate(flops=6 * 10**9, bytes_accessed=6 * 10**6, transcendentals=5 * 10**6),
        name="grads",
    )(
        queries[0], keys[0], values[0], prefix_keys, prefix_values, out_grad[0], boundaries, lengths, advantages
    )
    return outs[0][None], outs[1][None], outs[2][None], outs[3], outs[4]


def solution(mesh):
    in_specs = (
        P("dp", "ctx", None),
        P("dp", "ctx", None),
        P("dp", "ctx", None),
        P(),
        P(),
        P("dp", "ctx", None),
        P("dp", None),
        P("dp"),
        P("dp", None),
    )
    out_specs = (P("dp", "ctx", None), P("dp", "ctx", None), P("dp", "ctx", None), P(), P())
    return jax.shard_map(body, mesh=mesh, in_specs=in_specs, out_specs=out_specs, check_vma=False)
```

time: 1040 us -> 134 us (0.13)
  waiting for transfers between devices: 859 us -> 0 us
  Pallas kernels: 0 us -> 126 us
  local copies, waits for them, and re-layouts: 82.8 us -> 5.78 us
  matrix products: 69.3 us -> 0 us
  between operations: 14.7 us -> 1.31 us
    unnamed x7 -> x0, waiting for transfers between devices: 473 us -> none
    psum x1 -> x0, waiting for transfers between devices: 256 us -> none  [body(): lax.psum((prefix_key_part, prefix_value_part), ('dp', 'ctx'))]
    all_gather x2 -> x0, waiting for transfers between devices: 130 us -> none  [the longest x1 68.8 us: body(): lax.all_gather(values, 'ctx', axis=1, tiled=True)]
    pallas_call x0 -> x1, Pallas kernels: none -> 126 us  [body(): pl.pallas_call(kernel, out_shape=[jax.ShapeDtypeStruct((ROWS, width), BF1...]
    dot_general x112 -> x0, matrix products: 69.3 us -> none  [the longest x16 22.5 us: stats_update(): jnp.einsum('grk,kd->grd', raised.astype(jnp.bfloat16), value_rows, prefer...]
    unnamed x43 -> x13, local copies, waits for them, and re-layouts: 51.3 us -> 5.78 us
  transfers between devices with their start and end apart: 5 -> 0, of which waited for: 5 -> 0; matrix products, arithmetic and copies ran while one was open for 5% -> 0% of each run, Pallas kernels for 0% -> 0%
where the time goes in v1:
time: 134 us
  Pallas kernels  126 us (94%)
  local copies, waits for them, and re-layouts  5.78 us (4%)
    pallas_call x1, Pallas kernels, body(): pl.pallas_call(kernel, out_shape=[jax.ShapeDtypeStruct((ROWS, width), BF1...  126 us
    unnamed x13, local copies, waits for them, and re-layouts  5.78 us

profile of v1, /device:TPU:1, one launch (start us, length us, event | category | flops | bytes accessed | tf_op | source)
XLA Modules:
  0.0 133.6 jit_solution(14475230274745171261)
XLA Ops:
  1.3 126.5 %grads.1 = (bf16[128,4096]{1,0:T(8,128)(2,1)}, bf16[128,1024]{1,0:T(8,128)(2,1)}, bf16[128,1024]{1,0:T(8,128)(2,1)}, f32[128,1024]{1,0:T(8,128)}, f32[128,1024]{1,0:T(8,128)}) custom-call(bf16[128,4096]{1,0:T(8,128)(2,1)} %bitcast.10, bf16[128,1024]{1,0:T(8,128)(2,1)} %bitcast.12, bf16[128,1024]{1,0:T(8,128)(2,1)} %bitcast.13, bf16[128,1024]{1,0:T(8,128)(2,1)} %pk_ref.1, ...), custom_call_target="tpu_custom_call" | custom-call | flops 6000000000 | bytes 6000000 | tf_op jit(solution)/shard_map/grads/pallas_call | solution.py:376
  127.8 0.0 copy-start.3
  127.8 0.0 copy-start.2
  127.8 2.3 %copy.20 = bf16[1,128,4096]{2,1,0:T(8,128)(2,1)} copy(bf16[1,128,4096]{2,1,0:T(8,128)(2,1)} %bitcast.7) | data formatting | bytes 2097152
  130.1 0.0 copy-done.3
  130.1 0.0 copy-start.1
  130.1 0.7 copy.21
  130.9 0.0 copy-done.2
  130.9 0.7 copy.22
  131.6 0.0 copy-done.1
  131.6 0.0 copy-start
  131.6 0.8 copy.23
  132.4 0.4 copy-done
  132.8 0.8 copy.24
Async XLA Ops:
  127.8 2.4 %copy-start.3 = (bf16[128,1024]{1,0:T(8,128)(2,1)S(1)}, bf16[128,1024]{1,0:T(8,128)(2,1)}, u32[]{:S(2)}) copy-start(bf16[128,1024]{1,0:T(8,128)(2,1)} %get-tuple-element.11) | copy-start | bytes 786436
  127.8 3.1 %copy-start.2 = (bf16[128,1024]{1,0:T(8,128)(2,1)S(1)}, bf16[128,1024]{1,0:T(8,128)(2,1)}, u32[]{:S(2)}) copy-start(bf16[128,1024]{1,0:T(8,128)(2,1)} %get-tuple-element.12) | copy-start | bytes 786436
  130.1 1.4 %copy-start.1 = (f32[128,1024]{1,0:T(8,128)S(1)}, f32[128,1024]{1,0:T(8,128)}, u32[]{:S(2)}) copy-start(f32[128,1024]{1,0:T(8,128)} %get-tuple-element.23) | copy-start | bytes 1572868
  131.6 1.2 copy-start

commit v2 on v1

v2 whole, which is shorter than its diff:
```python
import functools

import jax
import jax.numpy as jnp
from jax import lax
from jax.experimental import pallas as pl
from jax.experimental.pallas import tpu as pltpu
from jax.sharding import PartitionSpec as P

HEADS = 32
KV_HEADS = 8
GROUP = HEADS // KV_HEADS
HEAD_DIM = 128
PREFIX = 128
ROWS = 128
STEPS = 8
SCALE = HEAD_DIM**-0.5
SCALE_LOG2 = SCALE * 1.4426950408889634
NEG = -1e30
MESH = pl.DeviceIdType.MESH
F32 = jnp.float32
BF16 = jnp.bfloat16
AHEAD = 3
SECOND = 1
BACK = 2
LAG = 4
OVER = (1, 3, 5, 7)
WINDOW = 3
EARLY = 4
TAIL = 7
CONTRACT_LAST = (((1,), (1,)), ((), ()))
CONTRACT_FIRST = (((0,), (0,)), ((), ()))
CONTRACT_INNER = (((1,), (0,)), ((), ()))


def head_grads(h, ctx, keys_seen, unmasked, q_ref, og_ref, weight, kv, dkv, dq_ref, s_ref, d_ref):
    width = GROUP * HEAD_DIM
    cols = [pl.ds(pl.multiple_of(h * width + g * HEAD_DIM, HEAD_DIM), HEAD_DIM) for g in range(GROUP)]
    queries = jnp.concatenate([q_ref[:, c] for c in cols], axis=0)
    grads = jnp.concatenate(
        [(og_ref[:, c].astype(F32) * weight[...]).astype(BF16) for c in cols], axis=0
    )
    key_rows = kv[0, h, 0:keys_seen]
    value_rows = kv[1, h, 0:keys_seen]
    scores = lax.dot_general(key_rows, queries, CONTRACT_LAST, preferred_element_type=F32)
    query_pos = ctx * ROWS + lax.broadcasted_iota(jnp.int32, (1, ROWS), 1)
    query_pos = jnp.concatenate([query_pos] * GROUP, axis=1)
    key_pos = unmasked - PREFIX + lax.broadcasted_iota(jnp.int32, (keys_seen - unmasked, 1), 0)
    free, bound = scores[0:unmasked], scores[unmasked:]
    bound = jnp.where(key_pos <= query_pos, bound, NEG)
    s_ref[0:unmasked] = free
    s_ref[unmasked:keys_seen] = bound
    peak = jnp.maximum(
        jnp.max(free, axis=0, keepdims=True), jnp.max(bound, axis=0, keepdims=True)
    )
    d_ref[0:keys_seen] = lax.dot_general(value_rows, grads, CONTRACT_LAST, preferred_element_type=F32)
    raised = jnp.exp2((s_ref[0:keys_seen] - peak) * SCALE_LOG2)
    s_ref[0:keys_seen] = raised
    total = jnp.sum(raised, axis=0, keepdims=True)
    inverse = 1.0 / total
    delta = jnp.sum(raised * d_ref[0:keys_seen], axis=0, keepdims=True) * inverse
    probs = s_ref[0:keys_seen] * inverse
    score_grad = (probs * (d_ref[0:keys_seen] - delta)).astype(BF16)
    value_part = lax.dot_general(probs.astype(BF16), grads, CONTRACT_INNER, preferred_element_type=F32)
    dkv[1, h, 0:keys_seen] = value_part.astype(BF16)
    key_part = lax.dot_general(score_grad, queries, CONTRACT_INNER, preferred_element_type=F32)
    dkv[0, h, 0:keys_seen] = (key_part * SCALE).astype(BF16)
    query_part = lax.dot_general(key_rows, score_grad, CONTRACT_FIRST, preferred_element_type=F32)
    for g in range(GROUP):
        dq_ref[:, cols[g]] = (query_part[:, g * ROWS : (g + 1) * ROWS].T * SCALE).astype(BF16)


def kernel(
    q_hbm, k_hbm, v_hbm, pk_hbm, pv_hbm, og_hbm, bounds_ref, len_ref, adv_ref,
    dq_hbm, dk_hbm, dv_hbm, pg_hbm,
    q_ref, og_ref, dq_ref, dk_ref, dv_ref,
    kv, dkv, rb, s_ref, d_ref, weight,
    pbuf, acc, zbuf, ybuf, piece, fin, pgb,
    in_sem, kv_in_sem, out_sem, dq_sem, dkv_sem,
    kv_send, kv_recv, kv_recv_v, g_send, g_recv, p_send, p_recv,
    z_send, z_recv, y_send, y_recv, za_send, za_recv, f_send, f_recv,
):
    dp = lax.axis_index("dp")
    ctx = lax.axis_index("ctx")
    y = ctx % 4
    hi = ctx // 4
    z = hi * 4 + dp // 8
    own = dp % 8
    base = dp - own
    up = (y + 1) % 4
    down = (y + 3) % 4
    far = (y + 2) % 4

    def at_ctx(target):
        return (dp, target)

    def at_hi(target):
        return (dp, 4 + target)

    def at_own(target):
        return (base + target, ctx)

    def at_z(target):
        return ((target % 4) * 8 + own, (target // 4) * 4 + y)

    barrier = pltpu.get_barrier_semaphore()
    for step in range(1, 8):
        pl.semaphore_signal(barrier, inc=1, device_id=at_ctx((ctx + step) % 8), device_id_type=MESH)
        pl.semaphore_signal(barrier, inc=1, device_id=at_own((own + step) % 8), device_id_type=MESH)
        if step != 4:
            pl.semaphore_signal(barrier, inc=1, device_id=at_z((z + step) % 8), device_id_type=MESH)

    mine = pl.ds(pl.multiple_of((1 + ctx) * ROWS, ROWS), ROWS)
    kv_in = []
    for h in range(KV_HEADS):
        cols = pl.ds(h * HEAD_DIM, HEAD_DIM)
        pairs = (
            (k_hbm.at[:, cols], kv.at[0, h, mine]),
            (v_hbm.at[:, cols], kv.at[1, h, mine]),
            (pk_hbm.at[:, cols], kv.at[0, h, pl.ds(0, PREFIX)]),
            (pv_hbm.at[:, cols], kv.at[1, h, pl.ds(0, PREFIX)]),
        )
        for i, (s, d) in enumerate(pairs):
            kv_in.append(pltpu.make_async_copy(s, d, kv_in_sem.at[h, i]))
    for c in kv_in:
        c.start()
    big_in = [
        pltpu.make_async_copy(q_hbm, q_ref, in_sem.at[0]),
        pltpu.make_async_copy(og_hbm, og_ref, in_sem.at[1]),
    ]
    for c in big_in:
        c.start()

    def copy(src, dst, send, recv, target):
        return pltpu.make_async_remote_copy(
            src_ref=src, dst_ref=dst, send_sem=send, recv_sem=recv, device_id=target, device_id_type=MESH
        )

    def rows_of(j):
        return pl.ds(pl.multiple_of((1 + j) * ROWS, ROWS), ROWS)

    def block(ref, h, j):
        return ref.at[:, h, rows_of(j)]

    def half(ref, side, h, j):
        return ref.at[side, h, rows_of(j)]

    for j in range(1, 8):

        @pl.when(jnp.logical_and(ctx < j, hi == j // 4))
        def _(j=j):
            for h in range(KV_HEADS):
                kv[:, h, (1 + j) * ROWS : (2 + j) * ROWS] = jnp.zeros((2, ROWS, HEAD_DIM), BF16)

    pos = ctx * ROWS + lax.broadcasted_iota(jnp.int32, (ROWS, HEAD_DIM), 0)
    token = jnp.full((ROWS, HEAD_DIM), adv_ref[0, 0], F32)
    for s in range(1, STEPS):
        token = jnp.where(pos >= bounds_ref[0, s], adv_ref[0, s], token)
    weight[...] = jnp.where(pos < len_ref[0], token, 0.0)
    for c in kv_in:
        c.wait()
    for c in big_in:
        c.wait()

    pl.semaphore_wait(barrier, 20)

    def full_kv(kind, j, target):
        return lambda h: copy(block(kv, h, j), block(kv, h, j), kv_send.at[h, kind], kv_recv.at[h, j], target)

    def key_half(kind, j, target):
        return lambda h: copy(half(kv, 0, h, j), half(kv, 0, h, j), kv_send.at[h, kind], kv_recv.at[h, j], target)

    def value_half(kind, j, target):
        return lambda h: copy(half(kv, 1, h, j), half(kv, 1, h, j), kv_send.at[h, kind], kv_recv_v.at[h, j], target)

    lo_own = [(y + d < 4, full_kv(d - 1, ctx, at_ctx((y + d) % 4))) for d in (1, 2, 3)]
    lo_cross = [(None, full_kv(3, ctx, at_hi(y)))]
    hi_own = [
        (y < 3, full_kv(0, ctx, at_hi(up))),
        (y == 0, full_kv(1, ctx, at_hi(3))),
    ]
    hi_near = [(None, full_kv(2, y, at_hi(up))), (None, full_kv(3, y, at_hi(down)))]
    hi_pass_down = [
        (jnp.logical_or(y == 0, y == 1), full_kv(4, down, at_hi(up))),
        (y == 3, key_half(4, down, at_hi(up))),
    ]
    hi_pass_up = [
        (y == 0, full_kv(5, up, at_hi(down))),
        (y == 1, value_half(5, up, at_hi(down))),
    ]
    hi_pass_own = [
        (y == 1, key_half(6, 4 + down, at_hi(up))),
        (y == 2, full_kv(6, 4 + down, at_hi(up))),
        (y == 3, value_half(7, 4 + up, at_hi(down))),
    ]
    hi_pass = hi_pass_down + hi_pass_up + hi_pass_own

    def full_term(kind, j, slot, sem, target):
        return lambda h: copy(block(dkv, h, j), rb.at[slot, :, h], g_send.at[h, kind], g_recv.at[h, sem], target)

    def half_term(kind, side, j, slot, sem, target):
        return lambda h: copy(
            half(dkv, side, h, j), rb.at[slot, side, h], g_send.at[h, kind], g_recv.at[h, sem], target
        )

    lo_terms = [
        (y + d >= 4, full_term(d - 1, (y + d) % 4, 4 - d, 4 - d, at_ctx((y + d) % 4))) for d in (1, 2, 3)
    ]
    hi_first = [
        (y == 0, half_term(0, 0, far, 4, 4, at_hi(up))),
        (y == 0, half_term(1, 1, far, 4, 5, at_hi(down))),
        (y == 1, full_term(0, far, 4, 4, at_hi(down))),
        (y == 2, full_term(0, far, 6, 8, at_hi(down))),
        (y == 3, full_term(0, far, 5, 6, at_hi(up))),
        (y == 2, half_term(2, 0, 4 + far, 5, 6, at_hi(up))),
        (y == 2, half_term(3, 1, 4 + far, 5, 7, at_hi(down))),
        (y == 3, full_term(2, 4 + far, 4, 4, at_hi(down))),
        (y == 3, full_term(5, 4 + down, 2, 2, at_hi(down))),
    ]
    to_up = [(None, full_term(6, up, 0, 0, at_hi(up)))]
    to_down = [(None, full_term(7, down, 1, 1, at_hi(down)))]
    own_up = [(y == 3, full_term(8, 4 + up, 3, 3, at_hi(up)))]
    own_down = [(jnp.logical_or(y == 1, y == 2), full_term(5, 4 + down, 2, 2, at_hi(down)))]
    hi_second = to_up + to_down + own_up + own_down
    hi_back = [(None, full_term(9, y, 0, 0, at_ctx(y)))]

    def prefix_made(h):
        slot = jnp.minimum((own - h + 7) % 8, 6)
        return copy(dkv.at[:, h, pl.ds(0, PREFIX)], pbuf.at[slot], p_send.at[h], p_recv.at[slot], at_own(h))

    def start(entries, h):
        for cond, make in entries:
            if cond is None:
                make(h).start()
            else:
                pl.when(cond)(lambda make=make: make(h).start())

    def wait_send(entries, h):
        for cond, make in entries:
            if cond is None:
                make(h).wait_send()
            else:
                pl.when(cond)(lambda make=make: make(h).wait_send())

    def kv_arrived(h, j):
        copy(block(kv, h, j), block(kv, h, j), kv_send.at[h, 0], kv_recv.at[h, j], at_ctx(ctx)).wait_recv()

    def halves_arrived(h, j):
        copy(half(kv, 0, h, j), half(kv, 0, h, j), kv_send.at[h, 0], kv_recv.at[h, j], at_ctx(ctx)).wait_recv()
        copy(half(kv, 1, h, j), half(kv, 1, h, j), kv_send.at[h, 0], kv_recv_v.at[h, j], at_ctx(ctx)).wait_recv()

    def term_arrived(h, slot, sem=None):
        sem = slot if sem is None else sem
        copy(rb.at[slot, :, h], rb.at[slot, :, h], g_send.at[h, 0], g_recv.at[h, sem], at_ctx(ctx)).wait_recv()

    def half_term_arrived(h, slot, side, sem):
        copy(
            rb.at[slot, side, h], rb.at[slot, side, h], g_send.at[h, 0], g_recv.at[h, sem], at_ctx(ctx)
        ).wait_recv()

    grads = functools.partial(
        head_grads, q_ref=q_ref, og_ref=og_ref, weight=weight, kv=kv, dkv=dkv, dq_ref=dq_ref, s_ref=s_ref, d_ref=d_ref
    )

    def dq_copy(h):
        cols = pl.ds(pl.multiple_of(h * GROUP * HEAD_DIM, HEAD_DIM), GROUP * HEAD_DIM)
        return pltpu.make_async_copy(dq_ref.at[:, cols], dq_hbm.at[:, cols], dq_sem.at[h])

    def dkv_copies(h):
        cols = pl.ds(pl.multiple_of(h * HEAD_DIM, HEAD_DIM), HEAD_DIM)
        return (
            pltpu.make_async_copy(dk_ref.at[:, cols], dk_hbm.at[:, cols], dkv_sem.at[h, 0]),
            pltpu.make_async_copy(dv_ref.at[:, cols], dv_hbm.at[:, cols], dkv_sem.at[h, 1]),
        )

    def after_grads(h):
        pl.when(own != h)(lambda: prefix_made(h).start())
        dq_copy(h).start()

    def finish(h):
        def store(total):
            cols = pl.ds(pl.multiple_of(h * HEAD_DIM, HEAD_DIM), HEAD_DIM)
            dk_ref[:, cols] = total[0].astype(BF16)
            dv_ref[:, cols] = total[1].astype(BF16)
            for c in dkv_copies(h):
                c.start()

        @pl.when(hi == 0)
        def _():
            term_arrived(h, 0)
            for d in (1, 2, 3):

                @pl.when(y + d < 4)
                def _(d=d):
                    term_arrived(h, d)

                @pl.when(y + d >= 4)
                def _(d=d):
                    rb[d, :, h] = jnp.zeros((2, ROWS, HEAD_DIM), BF16)

            total = dkv[:, h, mine].astype(F32)
            for slot in range(4):
                total = total + rb[slot, :, h].astype(F32)
            store(total)

        @pl.when(hi == 1)
        def _():
            @pl.when(y < 3)
            def _():
                term_arrived(h, 2)

            @pl.when(y == 3)
            def _():
                rb[2, :, h] = jnp.zeros((2, ROWS, HEAD_DIM), BF16)

            @pl.when(y == 0)
            def _():
                term_arrived(h, 3)

            @pl.when(y > 0)
            def _():
                rb[3, :, h] = jnp.zeros((2, ROWS, HEAD_DIM), BF16)

            store(dkv[:, h, mine].astype(F32) + rb[2, :, h].astype(F32) + rb[3, :, h].astype(F32))

    def eighth(ref, i):
        return ref.at[pl.ds(pl.multiple_of(i * 32, 32), 32)]

    z_out = [
        lambda d=d: copy(eighth(acc, (z + d) % 8), zbuf.at[7 - d], z_send.at[d - 1], z_recv.at[7 - d], at_z((z + d) % 8))
        for d in range(1, 8)
    ]
    y_out = [
        lambda d=d: copy(ybuf.at[y], ybuf.at[y], y_send.at[d - 1], y_recv.at[3 - d], at_ctx(hi * 4 + (y + d) % 4))
        for d in range(1, 4)
    ]
    za_out = [
        lambda d=d: copy(piece, eighth(fin, z), za_send.at[d - 1], za_recv.at[7 - d], at_z((z + d) % 8))
        for d in range(1, 8)
    ]
    f_out = [
        lambda d=d: copy(pgb.at[own], pgb.at[own], f_send.at[d - 1], f_recv.at[7 - d], at_own((own + d) % 8))
        for d in range(1, 8)
    ]

    def prefix_steps(t):
        @pl.when(t - own == OVER[0])
        def _():
            for slot in range(7):
                copy(pbuf.at[slot], pbuf.at[slot], p_send.at[0], p_recv.at[slot], at_own(own)).wait_recv()
            total = dkv[:, own, 0:PREFIX].astype(F32)
            for slot in range(7):
                total = total + pbuf[slot].astype(F32)
            acc[...] = total.reshape(2 * PREFIX, HEAD_DIM)
            for c in z_out:
                c().start()

        @pl.when(t - own == OVER[1])
        def _():
            for slot in range(7):
                copy(zbuf.at[slot], zbuf.at[slot], z_send.at[0], z_recv.at[slot], at_z(z)).wait_recv()
            total = acc[pl.ds(pl.multiple_of(z * 32, 32), 32)]
            for slot in range(7):
                total = total + zbuf[slot]
            ybuf[y] = total
            for c in y_out:
                c().start()

        @pl.when(t - own == OVER[2])
        def _():
            for d in (1, 2, 3):
                there = (y + d) % 4
                copy(ybuf.at[there], ybuf.at[there], y_send.at[0], y_recv.at[d - 1], at_ctx(ctx)).wait_recv()
            total = ((ybuf[0] + ybuf[1]) + ybuf[2]) + ybuf[3]
            piece[...] = total
            fin[pl.ds(pl.multiple_of(z * 32, 32), 32)] = total
            for c in za_out:
                c().start()

        @pl.when(t - own == OVER[3])
        def _():
            for d in range(1, 8):
                copy(piece, eighth(fin, (z + d) % 8), za_send.at[0], za_recv.at[d - 1], at_z(z)).wait_recv()
            pgb[own] = fin[...].astype(BF16)
            for c in f_out:
                c().start()

    def near(h):
        if EARLY == 0:
            start(hi_own, h)
        else:
            pl.when(h >= EARLY)(lambda: start(hi_own, h))
        kv_arrived(h, y)
        start(hi_near, h)

    def pass_on(h):
        kv_arrived(h, down)
        start(hi_pass_down, h)
        kv_arrived(h, up)
        start(hi_pass_up, h)
        pl.when(jnp.logical_or(y == 1, y == 2))(lambda: kv_arrived(h, 4 + down))
        pl.when(y == 3)(lambda: kv_arrived(h, 4))
        start(hi_pass_own, h)

    def all_here(h):
        pl.when(y == 0)(lambda: halves_arrived(h, far))
        pl.when(y > 0)(lambda: kv_arrived(h, far))
        pl.when(y == 2)(lambda: halves_arrived(h, 4))
        pl.when(y == 3)(lambda: kv_arrived(h, 5))
        pl.when(y == 3)(lambda: kv_arrived(h, 6))

    def add_half(side, h, j, slot, sem):
        half_term_arrived(h, slot, side, sem)
        rows = rows_of(j)
        dkv[side, h, rows] = (dkv[side, h, rows].astype(F32) + rb[slot, side, h].astype(F32)).astype(BF16)

    def add_full(h, j, slot, sem):
        term_arrived(h, slot, sem)
        rows = rows_of(j)
        dkv[:, h, rows] = (dkv[:, h, rows].astype(F32) + rb[slot, :, h].astype(F32)).astype(BF16)

    def first(h):
        start(hi_first, h)
        pl.when(y >= 2)(lambda: start(to_up, h))
        pl.when(y == 2)(lambda: start(to_down, h))

    def second(h):
        @pl.when(y == 0)
        def _():
            add_full(h, down, 4, 4)
            start(to_down, h)
            add_full(h, up, 5, 6)
            start(to_up, h)

        @pl.when(y == 1)
        def _():
            add_full(h, down, 6, 8)
            start(to_down, h)
            add_half(0, h, up, 4, 4)
            start(to_up, h)
            add_half(1, h, 4 + down, 5, 7)
            start(own_down, h)

        @pl.when(y == 2)
        def _():
            add_full(h, 4 + down, 4, 4)
            start(own_down, h)

        @pl.when(y == 3)
        def _():
            add_half(1, h, down, 4, 5)
            start(to_down, h)
            add_half(0, h, 4 + up, 5, 6)
            start(own_up, h)

    def back(h):
        term_arrived(h, 0)
        term_arrived(h, 1)
        rows = rows_of(y)
        total = dkv[:, h, rows].astype(F32) + rb[0, :, h].astype(F32) + rb[1, :, h].astype(F32)
        dkv[:, h, rows] = total.astype(BF16)
        start(hi_back, h)

    @pl.when(hi == 0)
    def _():
        for h in range(WINDOW):
            start(lo_cross, h)
        for h in range(KV_HEADS):
            start(lo_own, h)
        for h in range(WINDOW, KV_HEADS):
            wait_send(lo_cross, h - WINDOW)
            start(lo_cross, h)

    @pl.when(hi == 1)
    def _():
        for h in range(EARLY):
            start(hi_own, h)
        for h in range(AHEAD):
            near(h)
        for h in range(AHEAD - 1):
            pass_on(h)

    def step(t, c):
        @pl.when(jnp.logical_and(hi == 0, t < KV_HEADS))
        def _():
            for j in range(3):
                pl.when(j < ctx)(lambda j=j: kv_arrived(t, j))
            grads(t, ctx, 5 * ROWS, PREFIX)
            start(lo_terms, t)
            after_grads(t)

        @pl.when(hi == 1)
        def _():
            pl.when(t + AHEAD < KV_HEADS)(lambda: near(t + AHEAD))
            pl.when(t + AHEAD - 1 < KV_HEADS)(lambda: pass_on(t + AHEAD - 1))

            @pl.when(t < KV_HEADS)
            def _():
                all_here(t)
                grads(t, ctx, 9 * ROWS, 5 * ROWS)
                first(t)
                after_grads(t)

            pl.when(jnp.logical_and(t >= SECOND, t - SECOND < KV_HEADS))(lambda: second(t - SECOND))
            pl.when(jnp.logical_and(t >= BACK, t - BACK < KV_HEADS))(lambda: back(t - BACK))

        prefix_steps(t)
        pl.when(jnp.logical_and(t >= LAG, t - LAG < KV_HEADS))(lambda: finish(t - LAG))
        return c

    lax.fori_loop(0, KV_HEADS + TAIL, step, 0)

    for d in range(1, 8):
        there = (own + d) % 8
        copy(pgb.at[there], pgb.at[there], f_send.at[0], f_recv.at[d - 1], at_own(own)).wait_recv()
    out = pltpu.make_async_copy(pgb, pg_hbm, out_sem.at[0])
    out.start()

    for c in z_out + y_out + za_out + f_out:
        c().wait_send()

    def drain(h, c):
        pl.when(own != h)(lambda: prefix_made(h).wait_send())

        @pl.when(hi == 0)
        def _():
            wait_send(lo_own + lo_terms, h)
            pl.when(h >= KV_HEADS - WINDOW)(lambda: wait_send(lo_cross, h))

        @pl.when(hi == 1)
        def _():
            wait_send(hi_own + hi_near + hi_pass + hi_first + hi_second + hi_back, h)

        dq_copy(h).wait()
        for made in dkv_copies(h):
            made.wait()
        return c

    lax.fori_loop(0, KV_HEADS, drain, 0)
    out.wait()


def place_kernel(dq_in, dk_in, dv_in, pg_ref, dq_out, dk_out, dv_out, dpk_ref, dpv_ref, big, small, in_sem, out_sem):
    parts = []
    for i in range(4):
        rows = pl.ds(i * 32, 32)
        parts.append((dq_in.at[rows], big.at[rows], dq_out.at[rows]))
    parts.append((dk_in, small.at[0], dk_out))
    parts.append((dv_in, small.at[1], dv_out))
    loads = [pltpu.make_async_copy(s, m, in_sem.at[i]) for i, (s, m, d) in enumerate(parts)]
    stores = [pltpu.make_async_copy(m, d, out_sem.at[i]) for i, (s, m, d) in enumerate(parts)]
    for c in loads:
        c.start()
    for h in range(KV_HEADS):
        cols = slice(h * HEAD_DIM, (h + 1) * HEAD_DIM)
        dpk_ref[:, cols] = pg_ref[h, 0:PREFIX].astype(F32)
        dpv_ref[:, cols] = pg_ref[h, PREFIX:].astype(F32)
    for load, store in zip(loads, stores):
        load.wait()
        store.start()
    for c in stores:
        c.wait()


def body(queries, keys, values, prefix_keys, prefix_values, out_grad, boundaries, lengths, advantages):
    width, kv_width = queries.shape[2], keys.shape[2]
    vmem = pl.BlockSpec(memory_space=pltpu.VMEM)
    smem = pl.BlockSpec(memory_space=pltpu.SMEM)
    any_ = pl.BlockSpec(memory_space=pl.ANY)
    dma = pltpu.SemaphoreType.DMA
    key_rows = PREFIX + 8 * ROWS
    pair = (2, KV_HEADS, key_rows, HEAD_DIM)
    shapes = [
        jax.ShapeDtypeStruct((ROWS, width), BF16),
        jax.ShapeDtypeStruct((ROWS, kv_width), BF16),
        jax.ShapeDtypeStruct((ROWS, kv_width), BF16),
    ]
    prefix_shape = jax.ShapeDtypeStruct((PREFIX, kv_width), F32)
    outs = pl.pallas_call(
        kernel,
        out_shape=shapes + [jax.ShapeDtypeStruct((KV_HEADS, 2 * PREFIX, HEAD_DIM), BF16)],
        in_specs=[any_] * 6 + [smem] * 3,
        out_specs=[any_] * 4,
        scratch_shapes=[
            pltpu.VMEM((ROWS, width), BF16),
            pltpu.VMEM((ROWS, width), BF16),
            pltpu.VMEM((ROWS, width), BF16),
            pltpu.VMEM((ROWS, kv_width), BF16),
            pltpu.VMEM((ROWS, kv_width), BF16),
            pltpu.VMEM(pair, BF16),
            pltpu.VMEM(pair, BF16),
            pltpu.VMEM((7, 2, KV_HEADS, ROWS, HEAD_DIM), BF16),
            pltpu.VMEM((key_rows, GROUP * ROWS), F32),
            pltpu.VMEM((key_rows, GROUP * ROWS), F32),
            pltpu.VMEM((ROWS, HEAD_DIM), F32),
            pltpu.VMEM((7, 2, PREFIX, HEAD_DIM), BF16),
            pltpu.VMEM((2 * PREFIX, HEAD_DIM), F32),
            pltpu.VMEM((7, 32, HEAD_DIM), F32),
            pltpu.VMEM((4, 32, HEAD_DIM), F32),
            pltpu.VMEM((32, HEAD_DIM), F32),
            pltpu.VMEM((2 * PREFIX, HEAD_DIM), F32),
            pltpu.VMEM((KV_HEADS, 2 * PREFIX, HEAD_DIM), BF16),
            dma((2,)),
            dma((KV_HEADS, 4)),
            dma((1,)),
            dma((KV_HEADS,)),
            dma((KV_HEADS, 2)),
            dma((KV_HEADS, 8)),
            dma((KV_HEADS, 8)),
            dma((KV_HEADS, 8)),
            dma((KV_HEADS, 10)),
            dma((KV_HEADS, 9)),
            dma((KV_HEADS,)),
            dma((7,)),
            dma((7,)),
            dma((7,)),
            dma((3,)),
            dma((3,)),
            dma((7,)),
            dma((7,)),
            dma((7,)),
            dma((7,)),
        ],
        compiler_params=pltpu.CompilerParams(
            collective_id=0, has_side_effects=True, vmem_limit_bytes=56 * 2**20
        ),
        cost_estimate=pl.CostEstimate(flops=6 * 10**9, bytes_accessed=6 * 10**6, transcendentals=5 * 10**6),
        name="grads",
    )(
        queries[0], keys[0], values[0], prefix_keys, prefix_values, out_grad[0], boundaries, lengths, advantages
    )
    placed = pl.pallas_call(
        place_kernel,
        out_shape=shapes + [prefix_shape, prefix_shape],
        in_specs=[any_] * 3 + [vmem],
        out_specs=[any_] * 3 + [vmem] * 2,
        scratch_shapes=[
            pltpu.VMEM((ROWS, width), BF16),
            pltpu.VMEM((2, ROWS, kv_width), BF16),
            dma((6,)),
            dma((6,)),
        ],
        name="place",
    )(*outs)
    return placed[0][None], placed[1][None], placed[2][None], placed[3], placed[4]


def solution(mesh):
    in_specs = (
        P("dp", "ctx", None),
        P("dp", "ctx", None),
        P("dp", "ctx", None),
        P(),
        P(),
        P("dp", "ctx", None),
        P("dp", None),
        P("dp"),
        P("dp", None),
    )
    out_specs = (P("dp", "ctx", None), P("dp", "ctx", None), P("dp", "ctx", None), P(), P())
    return jax.shard_map(body, mesh=mesh, in_specs=in_specs, out_specs=out_specs, check_vma=False)
```

time: 134 us -> 112 us (0.84)
  Pallas kernels: 126 us -> 110 us
  local copies, waits for them, and re-layouts: 5.78 us -> 0 us
    pallas_call x1 -> x2, Pallas kernels: 126 us -> 110 us  [the longest x1 106 us: body(): pl.pallas_call(kernel, out_shape=shapes + [jax.ShapeDtypeStruct((KV_HEADS...]
    unnamed x13 -> x0, local copies, waits for them, and re-layouts: 5.78 us -> none
where the time goes in v2:
time: 112 us; the launch traced here: 111 us
  Pallas kernels  110 us (98%)
  between operations  1.29 us (1%)
    pallas_call x1, Pallas kernels, body(): pl.pallas_call(kernel, out_shape=shapes + [jax.ShapeDtypeStruct((KV_HEADS...  106 us
    pallas_call x1, Pallas kernels, body(): pl.pallas_call(place_kernel, out_shape=shapes + [prefix_shape, prefix_sha...  4.2 us

profile of v2, /device:TPU:1, one launch (start us, length us, event | category | flops | bytes accessed | tf_op | source)
XLA Modules:
  0.0 111.1 jit_solution(16309790934211004121)
XLA Ops:
  1.3 105.6 %grads.1 = (bf16[128,4096]{1,0:T(8,128)(2,1)}, bf16[128,1024]{1,0:T(8,128)(2,1)}, bf16[128,1024]{1,0:T(8,128)(2,1)}, bf16[8,256,128]{2,1,0:T(8,128)(2,1)}) custom-call(bf16[128,4096]{1,0:T(8,128)(2,1)} %bitcast.7, bf16[128,1024]{1,0:T(8,128)(2,1)} %bitcast.10, bf16[128,1024]{1,0:T(8,128)(2,1)} %bitcast.11, bf16[128,1024]{1,0:T(8,128)(2,1)} %pk_hbm.1, ...), custom_call_target="tpu_custom_call" | custom-call | flops 6000000000 | bytes 6000000 | tf_op jit(solution)/shard_map/grads/pallas_call | solution.py:579
  106.9 4.2 %place.1 = (bf16[128,4096]{1,0:T(8,128)(2,1)}, bf16[128,1024]{1,0:T(8,128)(2,1)}, bf16[128,1024]{1,0:T(8,128)(2,1)}, f32[128,1024]{1,0:T(8,128)}, f32[128,1024]{1,0:T(8,128)}) custom-call(bf16[128,4096]{1,0:T(8,128)(2,1)} %get-tuple-element.14.dq_in, bf16[128,1024]{1,0:T(8,128)(2,1)} %get-tuple-element.15.dk_in, bf16[128,1024]{1,0:T(8,128)(2,1)} %get-tuple-element.16.dv_in, ...), custom_call_target="tpu_custom_call" | custom-call | tf_op jit(solution)/shard_map/place/pallas_call | solution.py:632

commit v3 on v2

--- a/solution.py
+++ b/solution.py
@@ -21,12 +21,12 @@
 F32 = jnp.float32
 BF16 = jnp.bfloat16
 AHEAD = 3
-SECOND = 1
-BACK = 2
-LAG = 4
-OVER = (1, 3, 5, 7)
-WINDOW = 3
-EARLY = 4
+SECOND = 3
+BACK = 5
+LAG = 7
+OVER = 4
+WINDOW = 2
+EARLY = 8
 TAIL = 7
 CONTRACT_LAST = (((1,), (1,)), ((), ()))
 CONTRACT_FIRST = (((0,), (0,)), ((), ()))
@@ -343,8 +343,10 @@
         for d in range(1, 8)
     ]
 
+    over = jnp.maximum(own + 1, OVER)
+
     def prefix_steps(t):
-        @pl.when(t - own == OVER[0])
+        @pl.when(t == over + 0)
         def _():
             for slot in range(7):
                 copy(pbuf.at[slot], pbuf.at[slot], p_send.at[0], p_recv.at[slot], at_own(own)).wait_recv()
@@ -355,7 +357,7 @@
             for c in z_out:
                 c().start()
 
-        @pl.when(t - own == OVER[1])
+        @pl.when(t == over + 1)
         def _():
             for slot in range(7):
                 copy(zbuf.at[slot], zbuf.at[slot], z_send.at[0], z_recv.at[slot], at_z(z)).wait_recv()
@@ -366,7 +368,7 @@
             for c in y_out:
                 c().start()
 
-        @pl.when(t - own == OVER[2])
+        @pl.when(t == over + 2)
         def _():
             for d in (1, 2, 3):
                 there = (y + d) % 4
@@ -377,7 +379,7 @@
             for c in za_out:
                 c().start()
 
-        @pl.when(t - own == OVER[3])
+        @pl.when(t == over + 3)
         def _():
             for d in range(1, 8):
                 copy(piece, eighth(fin, (z + d) % 8), za_send.at[0], za_recv.at[d - 1], at_z(z)).wait_recv()
@@ -486,8 +488,8 @@
             for j in range(3):
                 pl.when(j < ctx)(lambda j=j: kv_arrived(t, j))
             grads(t, ctx, 5 * ROWS, PREFIX)
+            after_grads(t)
             start(lo_terms, t)
-            after_grads(t)
 
         @pl.when(hi == 1)
         def _():
@@ -498,8 +500,8 @@
             def _():
                 all_here(t)
                 grads(t, ctx, 9 * ROWS, 5 * ROWS)
+                after_grads(t)
                 first(t)
-                after_grads(t)
 
             pl.when(jnp.logical_and(t >= SECOND, t - SECOND < KV_HEADS))(lambda: second(t - SECOND))
             pl.when(jnp.logical_and(t >= BACK, t - BACK < KV_HEADS))(lambda: back(t - BACK))
@@ -540,10 +542,15 @@
     out.wait()
 
 
-def place_kernel(dq_in, dk_in, dv_in, pg_ref, dq_out, dk_out, dv_out, dpk_ref, dpv_ref, big, small, in_sem, out_sem):
+def place_kernel(
+    dq_in, dk_in, dv_in, pg_in, dq_out, dk_out, dv_out, dpk_out, dpv_out,
+    big, small, prefix, wide, in_sem, out_sem, prefix_in, prefix_out,
+):
+    fetch = pltpu.make_async_copy(pg_in, prefix, prefix_in.at[0])
+    fetch.start()
     parts = []
-    for i in range(4):
-        rows = pl.ds(i * 32, 32)
+    for i in range(2):
+        rows = pl.ds(i * 64, 64)
         parts.append((dq_in.at[rows], big.at[rows], dq_out.at[rows]))
     parts.append((dk_in, small.at[0], dk_out))
     parts.append((dv_in, small.at[1], dv_out))
@@ -551,20 +558,26 @@
     stores = [pltpu.make_async_copy(m, d, out_sem.at[i]) for i, (s, m, d) in enumerate(parts)]
     for c in loads:
         c.start()
+    fetch.wait()
     for h in range(KV_HEADS):
         cols = slice(h * HEAD_DIM, (h + 1) * HEAD_DIM)
-        dpk_ref[:, cols] = pg_ref[h, 0:PREFIX].astype(F32)
-        dpv_ref[:, cols] = pg_ref[h, PREFIX:].astype(F32)
+        wide[0, :, cols] = prefix[h, 0:PREFIX].astype(F32)
+        wide[1, :, cols] = prefix[h, PREFIX:].astype(F32)
+    puts = [
+        pltpu.make_async_copy(wide.at[0], dpk_out, prefix_out.at[0]),
+        pltpu.make_async_copy(wide.at[1], dpv_out, prefix_out.at[1]),
+    ]
+    for c in puts:
+        c.start()
     for load, store in zip(loads, stores):
         load.wait()
         store.start()
-    for c in stores:
+    for c in puts + stores:
         c.wait()
 
 
 def body(queries, keys, values, prefix_keys, prefix_values, out_grad, boundaries, lengths, advantages):
     width, kv_width = queries.shape[2], keys.shape[2]
-    vmem = pl.BlockSpec(memory_space=pltpu.VMEM)
     smem = pl.BlockSpec(memory_space=pltpu.SMEM)
     any_ = pl.BlockSpec(memory_space=pl.ANY)
     dma = pltpu.SemaphoreType.DMA
@@ -632,13 +645,17 @@
     placed = pl.pallas_call(
         place_kernel,
         out_shape=shapes + [prefix_shape, prefix_shape],
-        in_specs=[any_] * 3 + [vmem],
-        out_specs=[any_] * 3 + [vmem] * 2,
+        in_specs=[any_] * 4,
+        out_specs=[any_] * 5,
         scratch_shapes=[
             pltpu.VMEM((ROWS, width), BF16),
             pltpu.VMEM((2, ROWS, kv_width), BF16),
-            dma((6,)),
-            dma((6,)),
+            pltpu.VMEM((KV_HEADS, 2 * PREFIX, HEAD_DIM), BF16),
+            pltpu.VMEM((2, PREFIX, kv_width), F32),
+            dma((4,)),
+            dma((4,)),
+            dma((1,)),
+            dma((2,)),
         ],
         name="place",
     )(*outs)

time: 112 us -> 107 us (0.955)
  Pallas kernels: 110 us -> 104 us
    pallas_call x1, Pallas kernels: 106 us -> 101 us  [body(): pl.pallas_call(kernel, out_shape=shapes + [jax.ShapeDtypeStruct((KV_HEADS...]
where the time goes in v3:
time: 107 us; the launch traced here: 106 us
  Pallas kernels  104 us (97%)
  between operations  1.29 us (1%)
    pallas_call x1, Pallas kernels, body(): pl.pallas_call(kernel, out_shape=shapes + [jax.ShapeDtypeStruct((KV_HEADS...  101 us
    pallas_call x1, Pallas kernels, body(): pl.pallas_call(place_kernel, out_shape=shapes + [prefix_shape, prefix_sha...  3.13 us

profile of v3, /device:TPU:1, one launch (start us, length us, event | category | flops | bytes accessed | tf_op | source)
XLA Modules:
  0.0 105.7 jit_solution(2549025757067517341)
XLA Ops:
  1.3 101.2 %grads.1 = (bf16[128,4096]{1,0:T(8,128)(2,1)}, bf16[128,1024]{1,0:T(8,128)(2,1)}, bf16[128,1024]{1,0:T(8,128)(2,1)}, bf16[8,256,128]{2,1,0:T(8,128)(2,1)}) custom-call(bf16[128,4096]{1,0:T(8,128)(2,1)} %bitcast.7, bf16[128,1024]{1,0:T(8,128)(2,1)} %bitcast.10, bf16[128,1024]{1,0:T(8,128)(2,1)} %bitcast.11, bf16[128,1024]{1,0:T(8,128)(2,1)} %pk_hbm.1, ...), custom_call_target="tpu_custom_call" | custom-call | flops 6000000000 | bytes 6000000 | tf_op jit(solution)/shard_map/grads/pallas_call | solution.py:592
  102.5 3.1 %place.1 = (bf16[128,4096]{1,0:T(8,128)(2,1)}, bf16[128,1024]{1,0:T(8,128)(2,1)}, bf16[128,1024]{1,0:T(8,128)(2,1)}, f32[128,1024]{1,0:T(8,128)}, f32[128,1024]{1,0:T(8,128)}) custom-call(bf16[128,4096]{1,0:T(8,128)(2,1)} %get-tuple-element.14.dq_in, bf16[128,1024]{1,0:T(8,128)(2,1)} %get-tuple-element.15.dk_in, bf16[128,1024]{1,0:T(8,128)(2,1)} %get-tuple-element.16.dv_in, ...), custom_call_target="tpu_custom_call" | custom-call | tf_op jit(solution)/shard_map/place/pallas_call | solution.py:645

commit v4 on v3

--- a/solution.py
+++ b/solution.py
@@ -24,8 +24,8 @@
 SECOND = 3
 BACK = 5
 LAG = 7
-OVER = 4
-WINDOW = 2
+OVER = 5
+WINDOW = 1
 EARLY = 8
 TAIL = 7
 CONTRACT_LAST = (((1,), (1,)), ((), ()))
@@ -496,6 +496,8 @@
             pl.when(t + AHEAD < KV_HEADS)(lambda: near(t + AHEAD))
             pl.when(t + AHEAD - 1 < KV_HEADS)(lambda: pass_on(t + AHEAD - 1))
 
+            pl.when(jnp.logical_and(t >= SECOND, t - SECOND < KV_HEADS))(lambda: second(t - SECOND))
+            pl.when(jnp.logical_and(t >= BACK, t - BACK < KV_HEADS))(lambda: back(t - BACK))
             @pl.when(t < KV_HEADS)
             def _():
                 all_here(t)
@@ -503,8 +505,6 @@
                 after_grads(t)
                 first(t)
 
-            pl.when(jnp.logical_and(t >= SECOND, t - SECOND < KV_HEADS))(lambda: second(t - SECOND))
-            pl.when(jnp.logical_and(t >= BACK, t - BACK < KV_HEADS))(lambda: back(t - BACK))
 
         prefix_steps(t)
         pl.when(jnp.logical_and(t >= LAG, t - LAG < KV_HEADS))(lambda: finish(t - LAG))

time: 107 us -> 103 us (0.963)
  Pallas kernels: 104 us -> 101 us
    pallas_call x1, Pallas kernels: 101 us -> 98.1 us  [body(): pl.pallas_call(kernel, out_shape=shapes + [jax.ShapeDtypeStruct((KV_HEADS...]
where the time goes in v4:
time: 103 us
  Pallas kernels  101 us (98%)
  between operations  1.29 us (1%)
    pallas_call x1, Pallas kernels, body(): pl.pallas_call(kernel, out_shape=shapes + [jax.ShapeDtypeStruct((KV_HEADS...  98.1 us
    pallas_call x1, Pallas kernels, body(): pl.pallas_call(place_kernel, out_shape=shapes + [prefix_shape, prefix_sha...  3.13 us

profile of v4, /device:TPU:1, one launch (start us, length us, event | category | flops | bytes accessed | tf_op | source)
XLA Modules:
  0.0 102.5 jit_solution(17823544152954356545)
XLA Ops:
  1.3 98.1 %grads.1 = (bf16[128,4096]{1,0:T(8,128)(2,1)}, bf16[128,1024]{1,0:T(8,128)(2,1)}, bf16[128,1024]{1,0:T(8,128)(2,1)}, bf16[8,256,128]{2,1,0:T(8,128)(2,1)}) custom-call(bf16[128,4096]{1,0:T(8,128)(2,1)} %bitcast.7, bf16[128,1024]{1,0:T(8,128)(2,1)} %bitcast.10, bf16[128,1024]{1,0:T(8,128)(2,1)} %bitcast.11, bf16[128,1024]{1,0:T(8,128)(2,1)} %pk_hbm.1, ...), custom_call_target="tpu_custom_call" | custom-call | flops 6000000000 | bytes 6000000 | tf_op jit(solution)/shard_map/grads/pallas_call | solution.py:592
  99.4 3.1 %place.1 = (bf16[128,4096]{1,0:T(8,128)(2,1)}, bf16[128,1024]{1,0:T(8,128)(2,1)}, bf16[128,1024]{1,0:T(8,128)(2,1)}, f32[128,1024]{1,0:T(8,128)}, f32[128,1024]{1,0:T(8,128)}) custom-call(bf16[128,4096]{1,0:T(8,128)(2,1)} %get-tuple-element.14.dq_in, bf16[128,1024]{1,0:T(8,128)(2,1)} %get-tuple-element.15.dk_in, bf16[128,1024]{1,0:T(8,128)(2,1)} %get-tuple-element.16.dv_in, ...), custom_call_target="tpu_custom_call" | custom-call | tf_op jit(solution)/shard_map/place/pallas_call | solution.py:645
